TPU v7x, 32 devices: a whole 2x2x4 slice. The times are simulated.
32 devices in a mesh: groups: 2 (over y), trunk: 4 (over z), branch: 2 (over x), tensor: 2 (over core).
Axes of the slice: x: 2, y: 2, z: 4, core: 2. Of those that a mesh axis runs over, the one named last changes fastest.
Arguments:
- query: bfloat16 [4, 128, 4096], P(('groups', 'branch'), 'trunk', 'tensor'), parts along dimension 0, may hold values from -6 to 6
- cotangent: bfloat16 [4, 128, 4096], P(('groups', 'branch'), 'trunk', 'tensor'), parts along dimension 0, may hold values from -6 to 6
- branch_keys: bfloat16 [4, 128, 512], P(('groups', 'branch'), 'trunk', 'tensor'), parts along dimension 0, may hold values from -6 to 6
- rollout_value_rows: bfloat16 [4, 128, 512], P(('groups', 'branch'), 'trunk', 'tensor'), parts along dimension 0, may hold values from -6 to 6
- trunk_keys: bfloat16 [2048, 512], P(('groups', 'trunk', 'branch'), 'tensor'), parts along dimension 0, may hold values from -6 to 6
- shared_trunk_values: bfloat16 [2048, 512], P(('groups', 'trunk', 'branch'), 'tensor'), parts along dimension 0, may hold values from -6 to 6
- forks: int32 [4], P(('groups', 'branch')), parts along dimension 0, may hold values from 2 to 1024, as said below
- lengths: int32 [4], P(('groups', 'branch')), parts along dimension 0, may hold values from 32 to 128, as said below
Outputs:
- query_grad: bfloat16 [4, 128, 4096], P(('groups', 'branch'), 'trunk', 'tensor'), parts along dimension 0
- trunk_key_grad: bfloat16 [2048, 512], P(('groups', 'trunk', 'branch'), 'tensor'), parts along dimension 0
- trunk_value_grad: bfloat16 [2048, 512], P(('groups', 'trunk', 'branch'), 'tensor'), parts along dimension 0
- branch_key_grad: bfloat16 [4, 128, 512], P(('groups', 'branch'), 'trunk', 'tensor'), parts along dimension 0
- branch_value_grad: bfloat16 [4, 128, 512], P(('groups', 'branch'), 'trunk', 'tensor'), parts along dimension 0
There are 2 independent parts, one for each index of `groups`. A program takes and returns all parts, laid end to end along the dimension named above; each array names one. Nothing has to cross between parts.
Inputs may be any that keep to these rules, and one draw needn't show every extreme that they name: Some rollout forks at the end of the trunk in every draw. `lengths`: some rollout fills all 128 positions in every draw.
All inputs are finite; a program needn't handle non-finite values.
Results may differ from a plain program's by a relative error of at most 0.028.
Values may be sent and summed in bfloat16 or wider, within the bound.
A program may use at most 64 MiB of HBM per device.

v0:
```python
import jax
import jax.numpy as jnp
from jax import lax
from jax.sharding import PartitionSpec as P

HEAD_WIDTH = 128


def shards(
    query,
    cotangent,
    branch_keys,
    rollout_value_rows,
    trunk_keys,
    shared_trunk_values,
    forks,
    lengths,
):
    scale_factor = HEAD_WIDTH ** (-0.5)
    query_vectors, output_gradients = (
        lax.all_gather(query, "trunk", axis=1, tiled=True),
        lax.all_gather(cotangent, "trunk", axis=1, tiled=True),
    )
    slab_keys, slab_values = (
        lax.all_gather(trunk_keys, "branch", axis=0, tiled=True),
        lax.all_gather(shared_trunk_values, "branch", axis=0, tiled=True),
    )
    trunk_index = lax.axis_index("trunk")
    slab_rows = slab_keys.shape[0]
    block_rows = branch_keys.shape[1]
    seq_rows = query_vectors.shape[1]
    fork_point = forks[0]
    length = lengths[0]
    positions = jnp.arange(seq_rows, dtype=jnp.int32)
    is_valid = positions < length
    output_gradients = output_gradients[0] * is_valid[:, None].astype(jnp.bfloat16)
    keys_local = jnp.concatenate([slab_keys, branch_keys[0]], 0)
    values_local = jnp.concatenate([slab_values, rollout_value_rows[0]], 0)
    slab_positions = trunk_index * slab_rows + jnp.arange(slab_rows, dtype=jnp.int32)
    block_positions = trunk_index * block_rows + jnp.arange(block_rows, dtype=jnp.int32)
    trunk_seen = jnp.broadcast_to(slab_positions[None, :] < fork_point, (seq_rows, slab_rows))
    own_seen = (block_positions[None, :] <= positions[:, None]) & (
        block_positions[None, :] < length
    )
    visible = jnp.concatenate([trunk_seen, own_seen], 1)
    kv_heads = keys_local.shape[1] // HEAD_WIDTH
    q_heads = query_vectors.shape[2] // HEAD_WIDTH
    group_rollouts = q_heads // kv_heads
    head_queries = (
        query_vectors[0]
        .reshape(seq_rows, kv_heads, group_rollouts, HEAD_WIDTH)
        .transpose(1, 2, 0, 3)
    )
    gradient_heads = output_gradients.reshape(
        seq_rows, kv_heads, group_rollouts, HEAD_WIDTH
    ).transpose(1, 2, 0, 3)
    head_keys = keys_local.reshape(-1, kv_heads, HEAD_WIDTH).transpose(1, 0, 2)
    head_values = values_local.reshape(-1, kv_heads, HEAD_WIDTH).transpose(1, 0, 2)

    def scores_of(query_one, key_one):
        scores = (
            jnp.einsum("hsd,kd->hsk", query_one, key_one, preferred_element_type=jnp.float32)
            * scale_factor
        )
        return jnp.where(visible[None], scores, -1e30)

    def local_max(items):
        return jnp.max(scores_of(items[0], items[1]), -1)

    row_max = lax.pmax(lax.map(local_max, (head_queries, head_keys)), "trunk")

    def local_total(items):
        return jnp.sum(jnp.exp(scores_of(items[0], items[1]) - items[2][..., None]), -1)

    row_total = lax.psum(lax.map(local_total, (head_queries, head_keys, row_max)), "trunk")

    def probs_of(query_one, key_one, largest, total):
        return jnp.exp(scores_of(query_one, key_one) - largest[..., None]) / total[..., None]

    def local_delta(items):
        query_one, grad_one, key_one, value_one, largest, total = items
        probs = probs_of(query_one, key_one, largest, total)
        dprobs = jnp.einsum("hsd,kd->hsk", grad_one, value_one, preferred_element_type=jnp.float32)
        return jnp.sum(probs * dprobs, -1)

    stacked = (head_queries, gradient_heads, head_keys, head_values, row_max, row_total)
    delta = lax.psum(lax.map(local_delta, stacked), "trunk")

    def grads_of(items):
        query_one, grad_one, key_one, value_one, largest, total, delta_one = items
        probs = probs_of(query_one, key_one, largest, total)
        dprobs = jnp.einsum("hsd,kd->hsk", grad_one, value_one, preferred_element_type=jnp.float32)
        probs_low = probs.astype(jnp.bfloat16)
        dscores = (probs * (dprobs - delta_one[..., None]) * scale_factor).astype(jnp.bfloat16)
        key_gradient = jnp.einsum(
            "hsk,hsd->kd", dscores, query_one, preferred_element_type=jnp.float32
        )
        value_gradient = jnp.einsum(
            "hsk,hsd->kd", probs_low, grad_one, preferred_element_type=jnp.float32
        )
        return (dscores, key_gradient, value_gradient)

    def local_grads(items):
        dscores, key_gradient, value_gradient = grads_of(items)
        dquery = jnp.einsum("hsk,kd->hsd", dscores, items[2], preferred_element_type=jnp.float32)
        return (dquery, key_gradient, value_gradient)

    dquery, key_gradient, value_gradient = lax.map(local_grads, stacked + (delta,))
    dquery = dquery.transpose(2, 0, 1, 3).reshape(1, seq_rows, q_heads * HEAD_WIDTH)
    query_grad = lax.psum_scatter(
        dquery.astype(jnp.bfloat16), "trunk", scatter_dimension=1, tiled=True
    )
    key_gradient = key_gradient.transpose(1, 0, 2).reshape(-1, kv_heads * HEAD_WIDTH)
    value_gradient = value_gradient.transpose(1, 0, 2).reshape(-1, kv_heads * HEAD_WIDTH)
    trunk_key_grad, trunk_value_grad = (
        lax.psum_scatter(
            key_gradient[:slab_rows].astype(jnp.bfloat16), "branch", scatter_dimension=0, tiled=True
        ).astype(jnp.float32),
        lax.psum_scatter(
            value_gradient[:slab_rows].astype(jnp.bfloat16),
            "branch",
            scatter_dimension=0,
            tiled=True,
        ).astype(jnp.float32),
    )
    branch_key_grad = key_gradient[slab_rows:][None].astype(jnp.bfloat16)
    branch_value_grad = value_gradient[slab_rows:][None].astype(jnp.bfloat16)
    return (
        query_grad,
        trunk_key_grad.astype(jnp.bfloat16),
        trunk_value_grad.astype(jnp.bfloat16),
        branch_key_grad,
        branch_value_grad,
    )


def solution(mesh):
    return jax.shard_map(
        shards,
        mesh=mesh,
        in_specs=(
            P(("groups", "branch"), "trunk", "tensor"),
            P(("groups", "branch"), "trunk", "tensor"),
            P(("groups", "branch"), "trunk", "tensor"),
            P(("groups", "branch"), "trunk", "tensor"),
            P(("groups", "trunk", "branch"), "tensor"),
            P(("groups", "trunk", "branch"), "tensor"),
            P(("groups", "branch")),
            P(("groups", "branch")),
        ),
        out_specs=(
            P(("groups", "branch"), "trunk", "tensor"),
            P(("groups", "trunk", "branch"), "tensor"),
            P(("groups", "trunk", "branch"), "tensor"),
            P(("groups", "branch"), "trunk", "tensor"),
            P(("groups", "branch"), "trunk", "tensor"),
        ),
        check_vma=False,
    )
```

profile of v0, /device:TPU:0, one launch (start us, length us, event | category | flops | bytes accessed | tf_op | source)
XLA Modules:
  0.0 146.7 jit_solution(12745501833036336018)
XLA Ops:
  8.6 0.8 copy.64
  9.4 0.8 copy.65
  10.3 1.0 copy.42
  11.2 5.9 %all_gather.13 = bf16[256,256]{0,1:T(8,128)(2,1)S(1)} all-gather(bf16[128,256]{0,1:T(8,128)(2,1)S(1)} %copy.42), channel_id=1, replica_groups=mesh['groups'=2,'trunk'=4,'branch'=2,'tensor'=2] {'branch'}, dimensions={0}, use_global_device_ids=true | all-gather | bytes 196608 | tf_op jit(solution)/shard_map/all_gather | solution.py:25
  17.4 5.0 %all_gather.15 = bf16[256,256]{0,1:T(8,128)(2,1)S(1)} all-gather(bf16[128,256]{0,1:T(8,128)(2,1)S(1)} %copy.49), channel_id=1, replica_groups=mesh['groups'=2,'trunk'=4,'branch'=2,'tensor'=2] {'branch'}, dimensions={0}, use_global_device_ids=true | all-gather | bytes 196608 | tf_op jit(solution)/shard_map/all_gather | solution.py:26
  22.6 16.6 %all_gather.12 = bf16[1,128,2048]{2,1,0:T(8,128)(2,1)S(1)} all-gather(bf16[1,32,2048]{2,1,0:T(8,128)(2,1)S(1)} %copy-done), channel_id=1, replica_groups=mesh['groups'=2,'trunk'=4,'branch'=2,'tensor'=2] {'trunk'}, dimensions={1}, use_global_device_ids=true | all-gather | bytes 655360 | tf_op jit(solution)/shard_map/all_gather | solution.py:21
  40.0 0.7 while.44
  40.7 11.1 %pmax.7 = f32[2,8,128]{2,1,0:T(8,128)S(1)} all-reduce(f32[2,8,128]{2,1,0:T(8,128)S(1)} %get-tuple-element.175), channel_id=1, replica_groups=mesh['groups'=2,'trunk'=4,'branch'=2,'tensor'=2] {'trunk'}, use_global_device_ids=true, to_apply=%region_3.4 | all-reduce | flops 2048 | bytes 16384 | tf_op jit(solution)/shard_map/pmax | solution.py:70
  51.8 1.0 while.45
  51.8 0.4 fusion.96
  52.3 0.4 fusion.96
  52.8 8.7 %psum.14 = f32[2,8,128]{2,1,0:T(8,128)S(1)} all-reduce(f32[2,8,128]{2,1,0:T(8,128)S(1)} %get-tuple-element.176), channel_id=1, replica_groups=mesh['groups'=2,'trunk'=4,'branch'=2,'tensor'=2] {'trunk'}, use_global_device_ids=true, to_apply=%region_7.8 | all-reduce | flops 2048 | bytes 16384 | tf_op jit(solution)/shard_map/psum | solution.py:75
  61.5 14.8 %all_gather.14 = bf16[1,128,2048]{2,1,0:T(8,128)(2,1)S(1)} all-gather(bf16[1,32,2048]{2,1,0:T(8,128)(2,1)S(1)} %copy-done.1), channel_id=1, replica_groups=mesh['groups'=2,'trunk'=4,'branch'=2,'tensor'=2] {'trunk'}, dimensions={1}, use_global_device_ids=true | all-gather | bytes 655360 | tf_op jit(solution)/shard_map/all_gather | solution.py:22
  77.0 1.7 %while.46 = (s32[]{:T(128)}, f32[2,8,128]{2,1,0:T(8,128)S(1)}, pred[128,288]{0,1:T(8,128)(4,1)S(1)}, bf16[2,8,128,128]{3,2,1,0:T(8,128)(2,1)S(1)}, bf16[2,288,12...) while((s32[]{:T(128)}, f32[2,8,128]{2,1,0:T(8,128)S(1)}, ...), condition=%wide.region_10.11_spmd, body=%wide.region_8.10_spmd.sunk | while | flops 152763392 | bytes 3106933 | solution.py:87
  77.0 0.4 fusion.101
  77.8 0.4 fusion.101
  78.6 10.6 %psum.15 = f32[2,8,128]{2,1,0:T(8,128)S(1)} all-reduce(f32[2,8,128]{2,1,0:T(8,128)S(1)} %get-tuple-element.177), channel_id=1, replica_groups=mesh['groups'=2,'trunk'=4,'branch'=2,'tensor'=2] {'trunk'}, use_global_device_ids=true, to_apply=%region_11.12 | all-reduce | flops 2048 | bytes 16384 | tf_op jit(solution)/shard_map/psum | solution.py:87
  89.2 4.1 %while.47 = (s32[]{:T(128)}, bf16[2,8,128,128]{3,2,1,0:T(8,128)(2,1)S(1)}, bf16[2,288,128]{2,1,0:T(8,128)(2,1)S(1)}, bf16[2,288,128]{2,1,0:T(8,128)(2,1)S(1)}, p...) while((s32[]{:T(128)}, ...), condition=%wide.region_13.14_spmd, body=%wide.region_12.13_spmd.sunk | while | flops 380141568 | bytes 7476365 | solution.py:108
  89.3 0.4 fusion.113
  89.7 0.4 fusion.117
  90.8 0.5 fusion.115
  91.3 0.4 fusion.113
  91.8 0.4 fusion.117
  92.8 0.5 fusion.115
  93.3 0.6 copy_bitcast_fusion
  94.1 0.7 copy_bitcast_fusion.1
  95.2 1.0 convert_element_type.70
  96.2 0.6 convert_element_type.74
  96.9 0.6 convert_element_type.73
  97.5 5.1 %reduce-scatter.8.cloned.1.call-done = bf16[128,256]{1,0:T(8,128)(2,1)} async-done(((bf16[256,256]{1,0:T(8,128)(2,1)}), bf16[128,256]{1,0:T(8,128)(2,1)}) %reduce-scatter.8.cloned.1.call-update) | async-done | bytes 65552 | tf_op jit(solution)/shard_map/reduce_scatter | solution.py:119
  102.6 13.1 %reduce-scatter.6.cloned.1.call-done = bf16[128,256]{1,0:T(8,128)(2,1)} async-done(((bf16[256,256]{1,0:T(8,128)(2,1)}), bf16[128,256]{1,0:T(8,128)(2,1)}) %reduce-scatter.6.cloned.1.call-update) | async-done | bytes 65552 | tf_op jit(solution)/shard_map/reduce_scatter | solution.py:116
  115.6 24.6 %reduce-scatter.4.cloned.1.call-done = bf16[1,32,2048]{2,1,0:T(8,128)(2,1)} async-done(((bf16[1,128,2048]{2,1,0:T(8,128)(2,1)}), bf16[1,32,2048]{2,1,0:T(8,128)(2,1)}) %reduce-scatter.4.cloned.1.call-update) | async-done | bytes 131088 | tf_op jit(solution)/shard_map/reduce_scatter | solution.py:110
  (62 shorter events, 5.3 us)
Async XLA Ops:
  7.2 10.1 %copy-start.2 = (bf16[128,256]{1,0:T(8,128)(2,1)S(1)}, bf16[128,256]{1,0:T(8,128)(2,1)}, u32[]{:S(2)}) copy-start(bf16[128,256]{1,0:T(8,128)(2,1)} %param.21) | copy-start | bytes 196612
  7.2 15.4 %copy-start = (bf16[1,32,2048]{2,1,0:T(8,128)(2,1)S(1)}, bf16[1,32,2048]{2,1,0:T(8,128)(2,1)}, u32[]{:S(2)}) copy-start(bf16[1,32,2048]{2,1,0:T(8,128)(2,1)} %param.16) | copy-start | bytes 393220
  7.2 95.4 %reduce-scatter.8.cloned.1.call-start = ((), (), s32[]{:S(2)}) async-start(), calls=%async_computation.5 | async-start | bytes 196608 | tf_op jit(solution)/shard_map/reduce_scatter | solution.py:119
  51.8 9.7 %copy-start.1 = (bf16[1,32,2048]{2,1,0:T(8,128)(2,1)S(1)}, bf16[1,32,2048]{2,1,0:T(8,128)(2,1)}, u32[]{:S(2)}) copy-start(bf16[1,32,2048]{2,1,0:T(8,128)(2,1)} %param.17) | copy-start | bytes 393220
  94.0 21.6 %reduce-scatter.6.cloned.1.call-start = ((), (), s32[]{:S(2)}) async-start(), calls=%async_computation.4 | async-start | bytes 196608 | tf_op jit(solution)/shard_map/reduce_scatter | solution.py:116
  94.8 45.4 %reduce-scatter.4.cloned.1.call-start = ((), (), s32[]{:S(2)}) async-start(), calls=%async_computation.3 | async-start | bytes 655360 | tf_op jit(solution)/shard_map/reduce_scatter | solution.py:110
Sparse Core Ops, SparseCore 0:
  94.1 8.3 reduce-scatter.7
  105.3 10.2 reduce-scatter.5
  118.5 21.6 reduce-scatter.3
where the time goes:
time: 147 us
  blocking collectives  72.6 us (49%)
  waiting for transfers between devices  42.7 us (29%)
  between operations  15.3 us (10%)
  local copies, waits for them, and re-layouts  8.28 us (6%)
  matrix products  7.01 us (5%)
    reduce_scatter x1, waiting for transfers between devices, shards(): lax.psum_scatter(dquery.astype(jnp.bfloat16), 'trunk', scatter_dimension=...  24.6 us
    all_gather x1, blocking collectives, shards(): lax.all_gather(query, 'trunk', axis=1, tiled=True)  16.6 us
    all_gather x1, blocking collectives, shards(): lax.all_gather(cotangent, 'trunk', axis=1, tiled=True)  14.8 us
    reduce_scatter x1, waiting for transfers between devices, shards(): lax.psum_scatter(key_gradient[:slab_rows].astype(jnp.bfloat16), 'branch',...  13.1 us
    pmax x1, blocking collectives, shards(): row_max = lax.pmax(lax.map(local_max, (head_queries, head_keys)), 'trunk')  11.1 us
    psum x1, blocking collectives, shards(): delta = lax.psum(lax.map(local_delta, stacked), 'trunk')  10.6 us
    psum x1, blocking collectives, shards(): lax.psum(lax.map(local_total, (head_queries, head_keys, row_max)), 'trunk')  8.72 us
    all_gather x1, blocking collectives, shards(): lax.all_gather(trunk_keys, 'branch', axis=0, tiled=True)  5.87 us
  transfers between devices with their start and end apart: 3, of which 3 were waited for; matrix products, arithmetic and copies ran while one was open for 2% of the time, Pallas kernels for 0%

commit v1 on v0

--- a/solution.py
+++ b/solution.py
@@ -1,6 +1,8 @@
 import jax
 import jax.numpy as jnp
 from jax import lax
+from jax.experimental import pallas as pl
+from jax.experimental.pallas import tpu as pltpu
 from jax.sharding import PartitionSpec as P
 
 HEAD_WIDTH = 128
@@ -134,9 +136,392 @@
     )
 
 
+MESH = pl.DeviceIdType.MESH
+W = HEAD_WIDTH
+NT = (((1,), (1,)), ((), ()))
+TN = (((0,), (0,)), ((), ()))
+HIDDEN = -1e30
+
+
+def dot(lhs, rhs, dims=None):
+    if dims is None:
+        return jnp.dot(lhs, rhs, preferred_element_type=jnp.float32)
+    return lax.dot_general(lhs, rhs, dims, preferred_element_type=jnp.float32)
+
+
+def fused_kernel(
+    forks,
+    lengths,
+    query,
+    cotangent,
+    branch_keys,
+    branch_values,
+    trunk_keys,
+    trunk_values,
+    query_grad,
+    trunk_key_grad,
+    trunk_value_grad,
+    branch_key_grad,
+    branch_value_grad,
+    q_in,
+    c_in,
+    kv,
+    own,
+    q_rows,
+    c_rows,
+    scores,
+    dprobs,
+    dq_total,
+    mine,
+    x_out,
+    x_in,
+    z_out,
+    z_in,
+    own_out,
+    own_in,
+    dq_out,
+    local_sem,
+    z_send,
+    z_recv,
+    x_send,
+    x_recv,
+    back_send,
+    back_recv,
+):
+    z = lax.axis_index("trunk")
+    x = lax.axis_index("branch")
+    head = lax.rem(z, 2)
+    at = (z, z + 1 - 2 * head, lax.rem(z + 2, 4), 3 - z)
+    other_x = {"branch": 1 - x}
+    rows = query.shape[1]
+    slab = trunk_keys.shape[0]
+    group = query.shape[2] // 2 // W
+    wide = group * W
+    cols = 2 * group * rows
+    scale = W ** (-0.5)
+
+    def head_cols(index, width):
+        return pl.ds(pl.multiple_of(index * width, width), width)
+
+    barrier = pltpu.get_barrier_semaphore()
+    for d in (1, 2, 3):
+        pl.semaphore_signal(barrier, inc=1, device_id={"trunk": at[d]}, device_id_type=MESH)
+    pl.semaphore_signal(barrier, inc=1, device_id=other_x, device_id_type=MESH)
+    pl.semaphore_wait(barrier, 4)
+
+    def remote(src, dst, send, recv, device):
+        return pltpu.make_async_remote_copy(
+            src_ref=src,
+            dst_ref=dst,
+            send_sem=send,
+            recv_sem=recv,
+            device_id=device,
+            device_id_type=MESH,
+        )
+
+    mine_cols = head_cols(head, W)
+    x_copies = {}
+    first = []
+    for n, ref in enumerate((trunk_keys, trunk_values)):
+        first.append(
+            remote(
+                ref.at[:, mine_cols], kv.at[1, 0, n], x_send.at[0, n], x_recv.at[0, n], other_x
+            )
+        )
+    x_copies[0] = first
+    z_copies = {}
+    for d in (1, 2, 3):
+        sent = head_cols(lax.rem(at[d], 2), W)
+        to = {"trunk": at[d]}
+        z_copies[d] = [
+            remote(ref.at[:, sent], kv.at[0, d, n], z_send.at[d, n], z_recv.at[d, n], to)
+            for n, ref in enumerate((trunk_keys, trunk_values))
+        ] + [
+            remote(ref.at[0, :, sent], own.at[n, d], z_send.at[d, 2 + n], z_recv.at[d, 2 + n], to)
+            for n, ref in enumerate((branch_keys, branch_values))
+        ]
+    pair_cols = head_cols(1 - head, wide)
+    q_copies = [
+        remote(
+            ref.at[0, :, pair_cols], dst.at[1], z_send.at[0, n], z_recv.at[0, n], {"trunk": at[1]}
+        )
+        for n, (ref, dst) in enumerate(((query, q_in), (cotangent, c_in)))
+    ]
+    for copy in z_copies[1][:2] + x_copies[0] + z_copies[2][:2] + z_copies[3][:2]:
+        copy.start()
+    for copy in q_copies:
+        copy.start()
+    for d in (1, 2, 3):
+        for copy in z_copies[d][2:]:
+            copy.start()
+    local = []
+    for n, ref in enumerate((trunk_keys, trunk_values)):
+        local.append(pltpu.make_async_copy(ref.at[:, mine_cols], kv.at[0, 0, n], local_sem.at[n]))
+    for n, ref in enumerate((branch_keys, branch_values)):
+        local.append(
+            pltpu.make_async_copy(ref.at[0, :, mine_cols], own.at[n, 0], local_sem.at[2 + n])
+        )
+    for n, (ref, dst) in enumerate(((query, q_in), (cotangent, c_in))):
+        local.append(
+            pltpu.make_async_copy(
+                ref.at[0, :, head_cols(head, wide)], dst.at[0], local_sem.at[4 + n]
+            )
+        )
+    for copy in local:
+        copy.start()
+
+    for d in (1, 2, 3):
+        for copy in z_copies[d][:2]:
+            copy.wait_recv()
+        x_copies[d] = [
+            remote(kv.at[0, d], kv.at[1, d], x_send.at[d, 0], x_recv.at[d, 0], other_x)
+        ]
+        x_copies[d][0].start()
+    for copy in local:
+        copy.wait()
+    for copy in q_copies:
+        copy.wait_recv()
+
+    fork = forks[0]
+    length = lengths[0]
+    row_iota = lax.broadcasted_iota(jnp.int32, (rows, W), 0)
+    for e in (0, 1):
+        live = (row_iota + at[e] * rows < length).astype(jnp.float32)
+        for g in range(group):
+            start = (e * group + g) * rows
+            q_rows[start : start + rows, :] = q_in[e, :, g * W : (g + 1) * W]
+            part = c_in[e, :, g * W : (g + 1) * W].astype(jnp.float32) * live
+            c_rows[start : start + rows, :] = part.astype(jnp.bfloat16)
+
+    col = lax.broadcasted_iota(jnp.int32, (1, cols), 1)
+    half = group * rows
+    col_pos = jnp.where(col < half, at[0], at[1]) * rows + lax.rem(col, rows)
+    slab_iota = lax.broadcasted_iota(jnp.int32, (slab, 1), 0)
+
+    blocks = [(r, d) for r in (0, 1) for d in range(4)]
+    base_of = {block: i * slab for i, block in enumerate(blocks)}
+    own_base = len(blocks) * slab
+    own_rows = 4 * rows
+
+    def score(base, size, key, value, seen):
+        part = dot(key, q_rows[...], NT) * scale
+        part = jnp.where(seen, part, HIDDEN)
+        scores[base : base + size, :] = part
+        dprobs[base : base + size, :] = dot(value, c_rows[...], NT)
+        return jnp.max(part, 0, keepdims=True)
+
+    def trunk_score(r, d):
+        side = x if r == 0 else 1 - x
+        seen = slab_iota + (at[d] * 2 + side) * slab < fork
+        return score(base_of[r, d], slab, kv[r, d, 0], kv[r, d, 1], seen)
+
+    largest = trunk_score(0, 0)
+    for d in (1, 2, 3):
+        largest = jnp.maximum(largest, trunk_score(0, d))
+    for d in (1, 2, 3):
+        for copy in z_copies[d][2:]:
+            copy.wait_recv()
+    own_iota = lax.broadcasted_iota(jnp.int32, (rows, 1), 0)
+    own_pos = jnp.concatenate([own_iota + at[d] * rows for d in range(4)], 0)
+    own_key = own[0].reshape(own_rows, W)
+    own_value = own[1].reshape(own_rows, W)
+    largest = jnp.maximum(
+        largest,
+        score(
+            own_base, own_rows, own_key, own_value, (own_pos <= col_pos) & (own_pos < length)
+        ),
+    )
+    for d in range(4):
+        for copy in x_copies[d]:
+            copy.wait_recv()
+        largest = jnp.maximum(largest, trunk_score(1, d))
+
+    total = jnp.zeros((1, cols), jnp.float32)
+    delta = jnp.zeros((1, cols), jnp.float32)
+    for base in range(0, own_base + own_rows, W):
+        weights = jnp.exp(scores[base : base + W, :] - largest)
+        scores[base : base + W, :] = weights
+        total += jnp.sum(weights, 0, keepdims=True)
+        delta += jnp.sum(weights * dprobs[base : base + W, :], 0, keepdims=True)
+    inverse = 1.0 / total
+    delta = delta * inverse
+    dq_total[...] = jnp.zeros_like(dq_total)
+
+    def grads(base, size, key):
+        probs = scores[base : base + size, :] * inverse
+        low = probs.astype(jnp.bfloat16)
+        dscores = (probs * (dprobs[base : base + size, :] - delta) * scale).astype(jnp.bfloat16)
+        dq_total[...] += dot(key, dscores, TN)
+        return dot(dscores, q_rows[...]), dot(low, c_rows[...])
+
+    back = {}
+    for d in (3, 2, 1, 0):
+        pair = grads(base_of[1, d], slab, kv[1, d, 0])
+        for n in (0, 1):
+            x_out[d, n] = pair[n].astype(jnp.bfloat16)
+        back[d] = remote(x_out.at[d], x_in.at[d], back_send.at[d], back_recv.at[d], other_x)
+        back[d].start()
+    pair = grads(own_base, own_rows, own_key)
+    for n in (0, 1):
+        mine_part = pair[n].astype(jnp.bfloat16)
+        for d in range(4):
+            own_out[d, n] = mine_part[d * rows : (d + 1) * rows, :]
+    for d in (3, 2, 1):
+        back[4 + d] = remote(
+            own_out.at[d],
+            own_in.at[d],
+            back_send.at[4 + d],
+            back_recv.at[4 + d],
+            {"trunk": at[d]},
+        )
+        back[4 + d].start()
+    for d in (3, 2, 1, 0):
+        pair = grads(base_of[0, d], slab, kv[0, d, 0])
+        for n in (0, 1):
+            mine[d, n] = pair[n]
+    for d in (3, 2):
+        back[d].wait_recv()
+        z_out[d] = (mine[d] + x_in[d].astype(jnp.float32)).astype(jnp.bfloat16)
+        back[8 + d] = remote(
+            z_out.at[d], z_in.at[d], back_send.at[8 + d], back_recv.at[8 + d], {"trunk": at[d]}
+        )
+        back[8 + d].start()
+    dq = dq_total[...].T.astype(jnp.bfloat16)
+    for g in range(group):
+        dq_out[:, g * W : (g + 1) * W] = dq[half + g * rows : half + (g + 1) * rows, :]
+    back[4] = remote(
+        dq_out,
+        query_grad.at[0, :, head_cols(head, wide)],
+        back_send.at[4],
+        back_recv.at[4],
+        {"trunk": at[1]},
+    )
+    back[4].start()
+    back[1].wait_recv()
+    z_out[1] = (mine[1] + x_in[1].astype(jnp.float32)).astype(jnp.bfloat16)
+    back[9] = remote(
+        z_out.at[1], z_in.at[1], back_send.at[9], back_recv.at[9], {"trunk": at[1]}
+    )
+    back[9].start()
+    for g in range(group):
+        query_grad[0, :, pl.ds(pl.multiple_of(head * wide + g * W, W), W)] = dq[
+            g * rows : (g + 1) * rows, :
+        ]
+    back[0].wait_recv()
+    kept = mine[0] + x_in[0].astype(jnp.float32)
+    f32 = jnp.float32
+    theirs = head_cols(1 - head, W)
+    for d in (3, 2, 1):
+        back[4 + d].wait_recv()
+    for n, ref in enumerate((branch_key_grad, branch_value_grad)):
+        ref[0, :, mine_cols] = (own_out[0, n].astype(f32) + own_in[2, n].astype(f32)).astype(
+            jnp.bfloat16
+        )
+        ref[0, :, theirs] = (own_in[1, n].astype(f32) + own_in[3, n].astype(f32)).astype(
+            jnp.bfloat16
+        )
+    back[10].wait_recv()
+    for n, ref in enumerate((trunk_key_grad, trunk_value_grad)):
+        ref[:, mine_cols] = (kept[n] + z_in[2, n].astype(f32)).astype(jnp.bfloat16)
+    back[11].wait_recv()
+    back[9].wait_recv()
+    for n, ref in enumerate((trunk_key_grad, trunk_value_grad)):
+        ref[:, theirs] = (z_in[1, n].astype(f32) + z_in[3, n].astype(f32)).astype(jnp.bfloat16)
+    back[4].wait_recv()
+    for copy in q_copies + sum(z_copies.values(), []) + sum(x_copies.values(), []):
+        copy.wait_send()
+    for copy in back.values():
+        copy.wait_send()
+
+
+def fused(
+    query,
+    cotangent,
+    branch_keys,
+    rollout_value_rows,
+    trunk_keys,
+    shared_trunk_values,
+    forks,
+    lengths,
+):
+    rows = query.shape[1]
+    slab = trunk_keys.shape[0]
+    wide = query.shape[2] // 2
+    cols = 2 * rows * (wide // W)
+    keys = 8 * slab + 4 * rows
+    bf16, f32 = jnp.bfloat16, jnp.float32
+    smem = pl.BlockSpec(memory_space=pltpu.SMEM)
+    anywhere = pl.BlockSpec(memory_space=pl.ANY)
+    vmem = pl.BlockSpec(memory_space=pltpu.VMEM)
+
+    def like(a):
+        return jax.ShapeDtypeStruct(a.shape, a.dtype)
+
+    dma = pltpu.SemaphoreType.DMA
+    return pl.pallas_call(
+        fused_kernel,
+        out_shape=(
+            like(query),
+            like(trunk_keys),
+            like(shared_trunk_values),
+            like(branch_keys),
+            like(rollout_value_rows),
+        ),
+        in_specs=[smem] * 2 + [anywhere] * 6,
+        out_specs=(vmem,) * 5,
+        scratch_shapes=[
+            pltpu.VMEM((2, rows, wide), bf16),
+            pltpu.VMEM((2, rows, wide), bf16),
+            pltpu.VMEM((2, 4, 2, slab, W), bf16),
+            pltpu.VMEM((2, 4, rows, W), bf16),
+            pltpu.VMEM((cols, W), bf16),
+            pltpu.VMEM((cols, W), bf16),
+            pltpu.VMEM((keys, cols), f32),
+            pltpu.VMEM((keys, cols), f32),
+            pltpu.VMEM((W, cols), f32),
+            pltpu.VMEM((4, 2, slab, W), f32),
+            pltpu.VMEM((4, 2, slab, W), bf16),
+            pltpu.VMEM((4, 2, slab, W), bf16),
+            pltpu.VMEM((4, 2, slab, W), bf16),
+            pltpu.VMEM((4, 2, slab, W), bf16),
+            pltpu.VMEM((4, 2, rows, W), bf16),
+            pltpu.VMEM((4, 2, rows, W), bf16),
+            pltpu.VMEM((rows, wide), bf16),
+            dma((6,)),
+            dma((4, 4)),
+            dma((4, 4)),
+            dma((4, 2)),
+            dma((4, 2)),
+            dma((12,)),
+            dma((12,)),
+        ],
+        compiler_params=pltpu.CompilerParams(
+            collective_id=0, has_side_effects=True, vmem_limit_bytes=32 * 1024 * 1024
+        ),
+        cost_estimate=pl.CostEstimate(
+            flops=10 * keys * cols * W, bytes_accessed=2**20, transcendentals=keys * cols
+        ),
+    )(
+        forks,
+        lengths,
+        query,
+        cotangent,
+        branch_keys,
+        rollout_value_rows,
+        trunk_keys,
+        shared_trunk_values,
+    )
+
+
+def plan_of(mesh):
+    if mesh.shape["trunk"] == 4 and mesh.shape["branch"] == 2:
+        return fused
+    return shards
+
+
 def solution(mesh):
     return jax.shard_map(
-        shards,
+        plan_of(mesh),
         mesh=mesh,
         in_specs=(
             P(("groups", "branch"), "trunk", "tensor"),

time: 147 us -> 38.3 us (0.26)
  blocking collectives: 72.6 us -> 0 us
  waiting for transfers between devices: 42.7 us -> 0 us
  Pallas kernels: 0 us -> 28 us
  between operations: 15.3 us -> 1.95 us
  matrix products: 7.01 us -> 0 us
    reduce_scatter x3 -> x0, waiting for transfers between devices: 42.7 us -> none  [the longest x1 24.6 us: shards(): lax.psum_scatter(dquery.astype(jnp.bfloat16), 'trunk', scatter_dimension=...]
    all_gather x4 -> x0, blocking collectives: 42.2 us -> none  [the longest x1 16.6 us: shards(): lax.all_gather(query, 'trunk', axis=1, tiled=True)]
    pallas_call x0 -> x1, Pallas kernels: none -> 28 us  [fused(): pl.pallas_call(fused_kernel, out_shape=(like(query), like(trunk_keys), li...]
    psum x2 -> x0, blocking collectives: 19.3 us -> none  [the longest x1 10.6 us: shards(): delta = lax.psum(lax.map(local_delta, stacked), 'trunk')]
    pmax x1 -> x0, blocking collectives: 11.1 us -> none  [shards(): row_max = lax.pmax(lax.map(local_max, (head_queries, head_keys)), 'trunk')]
    dot_general x18 -> x0, matrix products: 7.01 us -> none  [the longest x8 3.28 us: scores_of(): jnp.einsum('hsd,kd->hsk', query_one, key_one, preferred_element_type=jnp....]
    unnamed x8 -> x17, local copies, waits for them, and re-layouts: 1.08 us -> 8.04 us
    convert_element_type x6 -> x0, local copies, waits for them, and re-layouts: 3.91 us -> none  [the longest x2 1.36 us: shards(): dquery.astype(jnp.bfloat16)]
  transfers between devices with their start and end apart: 3 -> 0, of which waited for: 3 -> 0; matrix products, arithmetic and copies ran while one was open for 2% -> 0% of each run, Pallas kernels for 0% -> 0%
where the time goes in v1:
time: 38.3 us; the launch traced here: 38 us
  Pallas kernels  28 us (73%)
  local copies, waits for them, and re-layouts  8.04 us (21%)
  between operations  1.95 us (5%)
    pallas_call x1, Pallas kernels, fused(): pl.pallas_call(fused_kernel, out_shape=(like(query), like(trunk_keys), li...  28 us
    unnamed x17, local copies, waits for them, and re-layouts  8.04 us

profile of v1, /device:TPU:0, one launch (start us, length us, event | category | flops | bytes accessed | tf_op | source)
XLA Modules:
  0.0 38.0 jit_solution(9086948360148262806)
XLA Ops:
  1.9 0.0 copy-start
  1.9 0.9 %copy-done = bf16[1,32,2048]{2,1,0:T(8,128)(2,1)S(1)} copy-done((bf16[1,32,2048]{2,1,0:T(8,128)(2,1)S(1)}, bf16[1,32,2048]{2,1,0:T(8,128)(2,1)}, u32[]{:S(2)}) %copy-start) | copy-done | bytes 131096
  2.8 0.0 copy-start.1
  2.8 0.9 %copy-done.1 = bf16[1,32,2048]{2,1,0:T(8,128)(2,1)S(1)} copy-done((bf16[1,32,2048]{2,1,0:T(8,128)(2,1)S(1)}, bf16[1,32,2048]{2,1,0:T(8,128)(2,1)}, u32[]{:S(2)}) %copy-start.1) | copy-done | bytes 131096
  3.7 0.0 copy-start.2
  3.7 0.8 %copy-done.2 = bf16[128,256]{1,0:T(8,128)(2,1)S(1)} copy-done((bf16[128,256]{1,0:T(8,128)(2,1)S(1)}, bf16[128,256]{1,0:T(8,128)(2,1)}, u32[]{:S(2)}) %copy-start.2) | copy-done | bytes 65560
  4.6 0.0 copy-start.3
  4.6 0.8 %copy-done.3 = bf16[128,256]{1,0:T(8,128)(2,1)S(1)} copy-done((bf16[128,256]{1,0:T(8,128)(2,1)S(1)}, bf16[128,256]{1,0:T(8,128)(2,1)}, u32[]{:S(2)}) %copy-start.3) | copy-done | bytes 65560
  5.4 0.0 copy-start.4
  5.4 0.7 %copy-done.4 = bf16[1,32,256]{2,1,0:T(8,128)(2,1)S(1)} copy-done((bf16[1,32,256]{2,1,0:T(8,128)(2,1)S(1)}, bf16[1,32,256]{2,1,0:T(8,128)(2,1)}, u32[]{:S(2)}) %copy-start.4) | copy-done | bytes 16408
  6.1 0.0 copy-start.5
  6.1 0.7 %copy-done.5 = bf16[1,32,256]{2,1,0:T(8,128)(2,1)S(1)} copy-done((bf16[1,32,256]{2,1,0:T(8,128)(2,1)S(1)}, bf16[1,32,256]{2,1,0:T(8,128)(2,1)}, u32[]{:S(2)}) %copy-start.5) | copy-done | bytes 16408
  6.9 28.0 %shard_map.119 = (bf16[1,32,2048]{2,1,0:T(8,128)(2,1)S(1)}, bf16[128,256]{1,0:T(8,128)(2,1)S(1)}, bf16[128,256]{1,0:T(8,128)(2,1)S(1)}, bf16[1,32,256]{2,1,0:T(8,128)(2,1)S(1)}, bf16[1,32,256]{2,1,0:T(8,128)(2,1)S(1)}) custom-call(s32[1]{0:T(128)S(6)} %copy.18.forks, s32[1]{0:T(128)S(6)} %copy.19.lengths, bf16[1,32,2048]{2,1,0:T(8,128)(2,1)S(1)} %copy-done, ...), custom_call_target="tpu_custom_call" | custom-call | flops 754974720 | bytes 1048576 | tf_op jit(solution)/shard_map/pallas_call | solution.py:461
  34.8 0.7 %copy.20 = bf16[1,32,2048]{2,1,0:T(8,128)(2,1)} copy(bf16[1,32,2048]{2,1,0:T(8,128)(2,1)S(1)} %get-tuple-element.10) | data formatting | bytes 262144
  35.5 0.6 %copy.21 = bf16[128,256]{1,0:T(8,128)(2,1)} copy(bf16[128,256]{1,0:T(8,128)(2,1)S(1)} %get-tuple-element.11) | data formatting | bytes 131072
  36.1 0.6 %copy.22 = bf16[128,256]{1,0:T(8,128)(2,1)} copy(bf16[128,256]{1,0:T(8,128)(2,1)S(1)} %get-tuple-element.12) | data formatting | bytes 131072
  36.8 0.6 %copy.23 = bf16[1,32,256]{2,1,0:T(8,128)(2,1)} copy(bf16[1,32,256]{2,1,0:T(8,128)(2,1)S(1)} %get-tuple-element.13) | data formatting | bytes 32768
  37.4 0.6 %copy.24 = bf16[1,32,256]{2,1,0:T(8,128)(2,1)} copy(bf16[1,32,256]{2,1,0:T(8,128)(2,1)S(1)} %get-tuple-element.14) | data formatting | bytes 32768
Async XLA Ops:
  1.9 0.9 %copy-start = (bf16[1,32,2048]{2,1,0:T(8,128)(2,1)S(1)}, bf16[1,32,2048]{2,1,0:T(8,128)(2,1)}, u32[]{:S(2)}) copy-start(bf16[1,32,2048]{2,1,0:T(8,128)(2,1)} %query.1) | copy-start | bytes 393220
  2.8 0.9 %copy-start.1 = (bf16[1,32,2048]{2,1,0:T(8,128)(2,1)S(1)}, bf16[1,32,2048]{2,1,0:T(8,128)(2,1)}, u32[]{:S(2)}) copy-start(bf16[1,32,2048]{2,1,0:T(8,128)(2,1)} %cotangent.1) | copy-start | bytes 393220
  3.7 0.8 %copy-start.2 = (bf16[128,256]{1,0:T(8,128)(2,1)S(1)}, bf16[128,256]{1,0:T(8,128)(2,1)}, u32[]{:S(2)}) copy-start(bf16[128,256]{1,0:T(8,128)(2,1)} %trunk_keys.1) | copy-start | bytes 196612
  4.6 0.8 %copy-start.3 = (bf16[128,256]{1,0:T(8,128)(2,1)S(1)}, bf16[128,256]{1,0:T(8,128)(2,1)}, u32[]{:S(2)}) copy-start(bf16[128,256]{1,0:T(8,128)(2,1)} %trunk_values.1) | copy-start | bytes 196612
  5.4 0.7 %copy-start.4 = (bf16[1,32,256]{2,1,0:T(8,128)(2,1)S(1)}, bf16[1,32,256]{2,1,0:T(8,128)(2,1)}, u32[]{:S(2)}) copy-start(bf16[1,32,256]{2,1,0:T(8,128)(2,1)} %branch_keys.1) | copy-start | bytes 49156
  6.1 0.7 %copy-start.5 = (bf16[1,32,256]{2,1,0:T(8,128)(2,1)S(1)}, bf16[1,32,256]{2,1,0:T(8,128)(2,1)}, u32[]{:S(2)}) copy-start(bf16[1,32,256]{2,1,0:T(8,128)(2,1)} %branch_values.1) | copy-start | bytes 49156

commit v2 on v1

--- a/solution.py
+++ b/solution.py
@@ -159,10 +159,8 @@
     trunk_keys,
     trunk_values,
     query_grad,
-    trunk_key_grad,
-    trunk_value_grad,
-    branch_key_grad,
-    branch_value_grad,
+    z_in,
+    own_in,
     q_in,
     c_in,
     kv,
@@ -176,9 +174,7 @@
     x_out,
     x_in,
     z_out,
-    z_in,
     own_out,
-    own_in,
     dq_out,
     local_sem,
     z_send,
@@ -375,63 +371,66 @@
             {"trunk": at[d]},
         )
         back[4 + d].start()
+    kept = [pltpu.make_async_copy(own_out.at[0], own_in.at[0], local_sem.at[0])]
+    kept[0].start()
     for d in (3, 2, 1, 0):
         pair = grads(base_of[0, d], slab, kv[0, d, 0])
         for n in (0, 1):
             mine[d, n] = pair[n]
-    for d in (3, 2):
+    dq = dq_total[...].T.astype(jnp.bfloat16)
+    for e in (1, 0):
+        for g in range(group):
+            start = e * half + g * rows
+            dq_out[e, :, g * W : (g + 1) * W] = dq[start : start + rows, :]
+    dq_cols = query_grad.at[0, :, head_cols(head, wide)]
+    back[4] = remote(dq_out.at[1], dq_cols, back_send.at[4], back_recv.at[4], {"trunk": at[1]})
+    back[4].start()
+    kept.append(pltpu.make_async_copy(dq_out.at[0], dq_cols, local_sem.at[1]))
+    kept[1].start()
+    for d in (3, 2, 1, 0):
         back[d].wait_recv()
         z_out[d] = (mine[d] + x_in[d].astype(jnp.float32)).astype(jnp.bfloat16)
-        back[8 + d] = remote(
-            z_out.at[d], z_in.at[d], back_send.at[8 + d], back_recv.at[8 + d], {"trunk": at[d]}
-        )
-        back[8 + d].start()
-    dq = dq_total[...].T.astype(jnp.bfloat16)
-    for g in range(group):
-        dq_out[:, g * W : (g + 1) * W] = dq[half + g * rows : half + (g + 1) * rows, :]
-    back[4] = remote(
-        dq_out,
-        query_grad.at[0, :, head_cols(head, wide)],
-        back_send.at[4],
-        back_recv.at[4],
-        {"trunk": at[1]},
-    )
-    back[4].start()
-    back[1].wait_recv()
-    z_out[1] = (mine[1] + x_in[1].astype(jnp.float32)).astype(jnp.bfloat16)
-    back[9] = remote(
-        z_out.at[1], z_in.at[1], back_send.at[9], back_recv.at[9], {"trunk": at[1]}
-    )
-    back[9].start()
-    for g in range(group):
-        query_grad[0, :, pl.ds(pl.multiple_of(head * wide + g * W, W), W)] = dq[
-            g * rows : (g + 1) * rows, :
-        ]
-    back[0].wait_recv()
-    kept = mine[0] + x_in[0].astype(jnp.float32)
-    f32 = jnp.float32
-    theirs = head_cols(1 - head, W)
+        if d == 0:
+            kept.append(pltpu.make_async_copy(z_out.at[0], z_in.at[0], local_sem.at[2]))
+            kept[2].start()
+        else:
+            back[8 + d] = remote(
+                z_out.at[d], z_in.at[d], back_send.at[8 + d], back_recv.at[8 + d], {"trunk": at[d]}
+            )
+            back[8 + d].start()
     for d in (3, 2, 1):
         back[4 + d].wait_recv()
-    for n, ref in enumerate((branch_key_grad, branch_value_grad)):
-        ref[0, :, mine_cols] = (own_out[0, n].astype(f32) + own_in[2, n].astype(f32)).astype(
-            jnp.bfloat16
-        )
-        ref[0, :, theirs] = (own_in[1, n].astype(f32) + own_in[3, n].astype(f32)).astype(
-            jnp.bfloat16
-        )
-    back[10].wait_recv()
-    for n, ref in enumerate((trunk_key_grad, trunk_value_grad)):
-        ref[:, mine_cols] = (kept[n] + z_in[2, n].astype(f32)).astype(jnp.bfloat16)
-    back[11].wait_recv()
-    back[9].wait_recv()
-    for n, ref in enumerate((trunk_key_grad, trunk_value_grad)):
-        ref[:, theirs] = (z_in[1, n].astype(f32) + z_in[3, n].astype(f32)).astype(jnp.bfloat16)
+        back[8 + d].wait_recv()
     back[4].wait_recv()
     for copy in q_copies + sum(z_copies.values(), []) + sum(x_copies.values(), []):
         copy.wait_send()
     for copy in back.values():
         copy.wait_send()
+    for copy in kept:
+        copy.wait()
+
+
+def owners_sum(
+    query_in,
+    z_in,
+    own_in,
+    query_grad,
+    trunk_key_grad,
+    trunk_value_grad,
+    branch_key_grad,
+    branch_value_grad,
+):
+    head = lax.rem(lax.axis_index("trunk"), 2)
+    f32 = jnp.float32
+    query_grad[...] = query_in[...]
+    for a, b, which in ((0, 2, head), (1, 3, 1 - head)):
+        at = pl.ds(pl.multiple_of(which * W, W), W)
+        for n, ref in enumerate((trunk_key_grad, trunk_value_grad)):
+            ref[:, at] = (z_in[a, n].astype(f32) + z_in[b, n].astype(f32)).astype(jnp.bfloat16)
+        for n, ref in enumerate((branch_key_grad, branch_value_grad)):
+            ref[0, :, at] = (own_in[a, n].astype(f32) + own_in[b, n].astype(f32)).astype(
+                jnp.bfloat16
+            )
 
 
 def fused(
@@ -458,17 +457,15 @@
         return jax.ShapeDtypeStruct(a.shape, a.dtype)
 
     dma = pltpu.SemaphoreType.DMA
-    return pl.pallas_call(
+    shares = pl.pallas_call(
         fused_kernel,
         out_shape=(
             like(query),
-            like(trunk_keys),
-            like(shared_trunk_values),
-            like(branch_keys),
-            like(rollout_value_rows),
+            jax.ShapeDtypeStruct((4, 2, slab, W), bf16),
+            jax.ShapeDtypeStruct((4, 2, rows, W), bf16),
         ),
         in_specs=[smem] * 2 + [anywhere] * 6,
-        out_specs=(vmem,) * 5,
+        out_specs=(anywhere,) * 3,
         scratch_shapes=[
             pltpu.VMEM((2, rows, wide), bf16),
             pltpu.VMEM((2, rows, wide), bf16),
@@ -483,10 +480,8 @@
             pltpu.VMEM((4, 2, slab, W), bf16),
             pltpu.VMEM((4, 2, slab, W), bf16),
             pltpu.VMEM((4, 2, slab, W), bf16),
-            pltpu.VMEM((4, 2, slab, W), bf16),
             pltpu.VMEM((4, 2, rows, W), bf16),
-            pltpu.VMEM((4, 2, rows, W), bf16),
-            pltpu.VMEM((rows, wide), bf16),
+            pltpu.VMEM((2, rows, wide), bf16),
             dma((6,)),
             dma((4, 4)),
             dma((4, 4)),
@@ -496,7 +491,7 @@
             dma((12,)),
         ],
         compiler_params=pltpu.CompilerParams(
-            collective_id=0, has_side_effects=True, vmem_limit_bytes=32 * 1024 * 1024
+            collective_id=0, has_side_effects=True, vmem_limit_bytes=60 * 1024 * 1024
         ),
         cost_estimate=pl.CostEstimate(
             flops=10 * keys * cols * W, bytes_accessed=2**20, transcendentals=keys * cols
@@ -511,6 +506,15 @@
         trunk_keys,
         shared_trunk_values,
     )
+    return pl.pallas_call(
+        owners_sum,
+        out_shape=tuple(
+            like(a) for a in (query, trunk_keys, shared_trunk_values, branch_keys, rollout_value_rows)
+        ),
+        in_specs=[vmem] * 3,
+        out_specs=(vmem,) * 5,
+        compiler_params=pltpu.CompilerParams(vmem_limit_bytes=60 * 1024 * 1024),
+    )(*shares)
 
 
 def plan_of(mesh):

time: 38.3 us -> 32.2 us (0.84)
  local copies, waits for them, and re-layouts: 8.04 us -> 0 us
  Pallas kernels: 28 us -> 30.1 us
    unnamed x17 -> x0, local copies, waits for them, and re-layouts: 8.04 us -> none
    pallas_call x1 -> x2, Pallas kernels: 28 us -> 30.1 us  [the longest x1 28.4 us: fused(): pl.pallas_call(fused_kernel, out_shape=(like(query), jax.ShapeDtypeStruct...]
where the time goes in v2:
time: 32.2 us; the launch traced here: 32 us
  Pallas kernels  30.1 us (93%)
  between operations  1.93 us (6%)
    pallas_call x1, Pallas kernels, fused(): pl.pallas_call(fused_kernel, out_shape=(like(query), jax.ShapeDtypeStruct...  28.4 us
    pallas_call x1, Pallas kernels, fused(): pl.pallas_call(owners_sum, out_shape=tuple((like(a) for a in (query, trun...  1.72 us

profile of v2, /device:TPU:0, one launch (start us, length us, event | category | flops | bytes accessed | tf_op | source)
XLA Modules:
  0.0 32.0 jit_solution(6011408021721819822)
XLA Ops:
  1.9 28.4 %shard_map.119 = (bf16[1,32,2048]{2,1,0:T(8,128)(2,1)}, bf16[4,2,128,128]{3,2,1,0:T(8,128)(2,1)}, bf16[4,2,32,128]{3,2,1,0:T(8,128)(2,1)}) custom-call(s32[1]{0:T(128)S(6)} %copy.13.forks, s32[1]{0:T(128)S(6)} %copy.14.lengths, bf16[1,32,2048]{2,1,0:T(8,128)(2,1)} %query.1, bf16[1,32,2048]{2,1,0:T(8,128)(2,1)} %cotangent.1, bf16[1,32,256]{2,1,0:T(8,128)(2,1)} %branch_keys.1, ...), custom_call_target="tpu_custom_call" | custom-call | flops 754974720 | bytes 1048576 | tf_op jit(solution)/shard_map/pallas_call | solution.py:460
  30.3 1.7 %shard_map.120 = (bf16[1,32,2048]{2,1,0:T(8,128)(2,1)}, bf16[128,256]{1,0:T(8,128)(2,1)}, bf16[128,256]{1,0:T(8,128)(2,1)}, bf16[1,32,256]{2,1,0:T(8,128)(2,1)}, bf16[1,32,256]{2,1,0:T(8,128)(2,1)}) custom-call(bf16[1,32,2048]{2,1,0:T(8,128)(2,1)} %get-tuple-element.8.query_in, bf16[4,2,128,128]{3,2,1,0:T(8,128)(2,1)} %get-tuple-element.9.z_in, ...), custom_call_target="tpu_custom_call" | custom-call | tf_op jit(solution)/shard_map/pallas_call | solution.py:509

commit v3 on v2

--- a/solution.py
+++ b/solution.py
@@ -1,3 +1,5 @@
+import functools
+
 import jax
 import jax.numpy as jnp
 from jax import lax
@@ -161,8 +163,10 @@
     query_grad,
     z_in,
     own_in,
+    kv_here,
+    q_here,
+    own_here,
     q_in,
-    c_in,
     kv,
     own,
     q_rows,
@@ -176,6 +180,8 @@
     z_out,
     own_out,
     dq_out,
+    limits_out,
+    limits_in,
     local_sem,
     z_send,
     z_recv,
@@ -186,9 +192,12 @@
 ):
     z = lax.axis_index("trunk")
     x = lax.axis_index("branch")
+    core = lax.axis_index("tensor")
     head = lax.rem(z, 2)
     at = (z, z + 1 - 2 * head, lax.rem(z + 2, 4), 3 - z)
-    other_x = {"branch": 1 - x}
+    workers = [{"trunk": there, "branch": core, "tensor": 1 - x} for there in at]
+    homes = [{"trunk": there, "branch": 1 - core, "tensor": x} for there in at]
+    twin = {"tensor": 1 - core}
     rows = query.shape[1]
     slab = trunk_keys.shape[0]
     group = query.shape[2] // 2 // W
@@ -199,11 +208,23 @@
     def head_cols(index, width):
         return pl.ds(pl.multiple_of(index * width, width), width)
 
+    local = []
+    for i in (0, 1):
+        for n, ref in enumerate((trunk_keys, trunk_values)):
+            local.append((ref.at[:, pl.ds(i * W, W)], kv_here.at[i, n]))
+        for n, ref in enumerate((query, cotangent)):
+            local.append((ref.at[0, :, pl.ds(i * wide, wide)], q_here.at[i, n]))
+        for n, ref in enumerate((branch_keys, branch_values)):
+            local.append((ref.at[0, :, pl.ds(i * W, W)], own_here.at[i, n]))
+    local = [
+        pltpu.make_async_copy(src, dst, local_sem.at[k]) for k, (src, dst) in enumerate(local)
+    ]
+    for copy in local:
+        copy.start()
     barrier = pltpu.get_barrier_semaphore()
-    for d in (1, 2, 3):
-        pl.semaphore_signal(barrier, inc=1, device_id={"trunk": at[d]}, device_id_type=MESH)
-    pl.semaphore_signal(barrier, inc=1, device_id=other_x, device_id_type=MESH)
-    pl.semaphore_wait(barrier, 4)
+    for device in workers + homes:
+        pl.semaphore_signal(barrier, inc=1, device_id=device, device_id_type=MESH)
+    pl.semaphore_wait(barrier, len(workers + homes))
 
     def remote(src, dst, send, recv, device):
         return pltpu.make_async_remote_copy(
@@ -215,78 +236,51 @@
             device_id_type=MESH,
         )
 
-    mine_cols = head_cols(head, W)
-    x_copies = {}
-    first = []
-    for n, ref in enumerate((trunk_keys, trunk_values)):
-        first.append(
-            remote(
-                ref.at[:, mine_cols], kv.at[1, 0, n], x_send.at[0, n], x_recv.at[0, n], other_x
+    limits_out[0] = jnp.full(limits_out.shape[1:], forks[0], jnp.int32)
+    limits_out[1] = jnp.full(limits_out.shape[1:], lengths[0], jnp.int32)
+    z_copies = {}
+    for d in range(4):
+        sent = lax.rem(at[d], 2)
+        z_copies[d] = [
+            remote(here.at[sent], there(d), z_send.at[d, n], z_recv.at[d, n], workers[d])
+            for n, (here, there) in enumerate(
+                (
+                    (kv_here, lambda d: kv.at[0, :, d]),
+                    (own_here, lambda d: own.at[:, d]),
+                    (q_here, lambda d: q_in.at[d]),
+                )
             )
-        )
-    x_copies[0] = first
-    z_copies = {}
-    for d in (1, 2, 3):
-        sent = head_cols(lax.rem(at[d], 2), W)
-        to = {"trunk": at[d]}
-        z_copies[d] = [
-            remote(ref.at[:, sent], kv.at[0, d, n], z_send.at[d, n], z_recv.at[d, n], to)
-            for n, ref in enumerate((trunk_keys, trunk_values))
-        ] + [
-            remote(ref.at[0, :, sent], own.at[n, d], z_send.at[d, 2 + n], z_recv.at[d, 2 + n], to)
-            for n, ref in enumerate((branch_keys, branch_values))
+            if n < 2 or d < 2
         ]
-    pair_cols = head_cols(1 - head, wide)
-    q_copies = [
-        remote(
-            ref.at[0, :, pair_cols], dst.at[1], z_send.at[0, n], z_recv.at[0, n], {"trunk": at[1]}
-        )
-        for n, (ref, dst) in enumerate(((query, q_in), (cotangent, c_in)))
-    ]
-    for copy in z_copies[1][:2] + x_copies[0] + z_copies[2][:2] + z_copies[3][:2]:
-        copy.start()
-    for copy in q_copies:
-        copy.start()
-    for d in (1, 2, 3):
-        for copy in z_copies[d][2:]:
-            copy.start()
-    local = []
-    for n, ref in enumerate((trunk_keys, trunk_values)):
-        local.append(pltpu.make_async_copy(ref.at[:, mine_cols], kv.at[0, 0, n], local_sem.at[n]))
-    for n, ref in enumerate((branch_keys, branch_values)):
-        local.append(
-            pltpu.make_async_copy(ref.at[0, :, mine_cols], own.at[n, 0], local_sem.at[2 + n])
-        )
-    for n, (ref, dst) in enumerate(((query, q_in), (cotangent, c_in))):
-        local.append(
-            pltpu.make_async_copy(
-                ref.at[0, :, head_cols(head, wide)], dst.at[0], local_sem.at[4 + n]
-            )
-        )
-    for copy in local:
-        copy.start()
-
-    for d in (1, 2, 3):
-        for copy in z_copies[d][:2]:
-            copy.wait_recv()
-        x_copies[d] = [
-            remote(kv.at[0, d], kv.at[1, d], x_send.at[d, 0], x_recv.at[d, 0], other_x)
-        ]
-        x_copies[d][0].start()
+    limits = remote(limits_out, limits_in, z_send.at[2, 2], z_recv.at[2, 2], workers[0])
     for copy in local:
         copy.wait()
-    for copy in q_copies:
-        copy.wait_recv()
-
-    fork = forks[0]
-    length = lengths[0]
+    limits.start()
+    for d in (1, 2, 3, 0):
+        z_copies[d][0].start()
+    for d in (1, 2, 3, 0):
+        z_copies[d][1].start()
+    for d in (1, 0):
+        z_copies[d][2].start()
+
+    x_copies = {}
+    for d in (1, 2, 3, 0):
+        z_copies[d][0].wait_recv()
+        x_copies[d] = remote(kv.at[0, :, d], kv.at[1, :, d], x_send.at[d], x_recv.at[d], twin)
+        x_copies[d].start()
+    limits.wait_recv()
+    for e in (0, 1):
+        z_copies[e][2].wait_recv()
+
+    fork = limits_in[0, 0:1, 0:1]
+    length = limits_in[1, 0:1, 0:1]
     row_iota = lax.broadcasted_iota(jnp.int32, (rows, W), 0)
     for e in (0, 1):
         live = (row_iota + at[e] * rows < length).astype(jnp.float32)
         for g in range(group):
             start = (e * group + g) * rows
-            q_rows[start : start + rows, :] = q_in[e, :, g * W : (g + 1) * W]
-            part = c_in[e, :, g * W : (g + 1) * W].astype(jnp.float32) * live
+            q_rows[start : start + rows, :] = q_in[e, 0, :, g * W : (g + 1) * W]
+            part = q_in[e, 1, :, g * W : (g + 1) * W].astype(jnp.float32) * live
             c_rows[start : start + rows, :] = part.astype(jnp.bfloat16)
 
     col = lax.broadcasted_iota(jnp.int32, (1, cols), 1)
@@ -294,9 +288,7 @@
     col_pos = jnp.where(col < half, at[0], at[1]) * rows + lax.rem(col, rows)
     slab_iota = lax.broadcasted_iota(jnp.int32, (slab, 1), 0)
 
-    blocks = [(r, d) for r in (0, 1) for d in range(4)]
-    base_of = {block: i * slab for i, block in enumerate(blocks)}
-    own_base = len(blocks) * slab
+    own_base = 8 * slab
     own_rows = 4 * rows
 
     def score(base, size, key, value, seen):
@@ -306,17 +298,15 @@
         dprobs[base : base + size, :] = dot(value, c_rows[...], NT)
         return jnp.max(part, 0, keepdims=True)
 
-    def trunk_score(r, d):
-        side = x if r == 0 else 1 - x
-        seen = slab_iota + (at[d] * 2 + side) * slab < fork
-        return score(base_of[r, d], slab, kv[r, d, 0], kv[r, d, 1], seen)
-
-    largest = trunk_score(0, 0)
-    for d in (1, 2, 3):
-        largest = jnp.maximum(largest, trunk_score(0, d))
-    for d in (1, 2, 3):
-        for copy in z_copies[d][2:]:
-            copy.wait_recv()
+    def trunk_score(r):
+        side = 1 - core if r == 0 else core
+        pos = jnp.concatenate([slab_iota + (there * 2 + side) * slab for there in at], 0)
+        key, value = [kv[r, n].reshape(4 * slab, W) for n in (0, 1)]
+        return score(r * 4 * slab, 4 * slab, key, value, pos < fork)
+
+    largest = trunk_score(0)
+    for d in range(4):
+        z_copies[d][1].wait_recv()
     own_iota = lax.broadcasted_iota(jnp.int32, (rows, 1), 0)
     own_pos = jnp.concatenate([own_iota + at[d] * rows for d in range(4)], 0)
     own_key = own[0].reshape(own_rows, W)
@@ -327,10 +317,9 @@
             own_base, own_rows, own_key, own_value, (own_pos <= col_pos) & (own_pos < length)
         ),
     )
-    for d in range(4):
-        for copy in x_copies[d]:
-            copy.wait_recv()
-        largest = jnp.maximum(largest, trunk_score(1, d))
+    for d in (1, 2, 3, 0):
+        x_copies[d].wait_recv()
+    largest = jnp.maximum(largest, trunk_score(1))
 
     total = jnp.zeros((1, cols), jnp.float32)
     delta = jnp.zeros((1, cols), jnp.float32)
@@ -352,62 +341,58 @@
 
     back = {}
     for d in (3, 2, 1, 0):
-        pair = grads(base_of[1, d], slab, kv[1, d, 0])
+        if d in (3, 1):
+            key = kv[1, 0, d - 1 : d + 1].reshape(2 * slab, W)
+            pair = grads((3 + d) * slab, 2 * slab, key)
         for n in (0, 1):
-            x_out[d, n] = pair[n].astype(jnp.bfloat16)
-        back[d] = remote(x_out.at[d], x_in.at[d], back_send.at[d], back_recv.at[d], other_x)
+            part = pair[n][d % 2 * slab : (d % 2 + 1) * slab]
+            x_out[d, n] = part.astype(jnp.bfloat16)
+        back[d] = remote(x_out.at[d], x_in.at[d], back_send.at[d], back_recv.at[d], twin)
         back[d].start()
     pair = grads(own_base, own_rows, own_key)
     for n in (0, 1):
         mine_part = pair[n].astype(jnp.bfloat16)
         for d in range(4):
             own_out[d, n] = mine_part[d * rows : (d + 1) * rows, :]
-    for d in (3, 2, 1):
+    for d in (3, 2, 1, 0):
         back[4 + d] = remote(
-            own_out.at[d],
-            own_in.at[d],
-            back_send.at[4 + d],
-            back_recv.at[4 + d],
-            {"trunk": at[d]},
+            own_out.at[d], own_in.at[d], back_send.at[4 + d], back_recv.at[4 + d], homes[d]
         )
         back[4 + d].start()
-    kept = [pltpu.make_async_copy(own_out.at[0], own_in.at[0], local_sem.at[0])]
-    kept[0].start()
-    for d in (3, 2, 1, 0):
-        pair = grads(base_of[0, d], slab, kv[0, d, 0])
+    pair = grads(0, 4 * slab, kv[0, 0].reshape(4 * slab, W))
+    for d in range(4):
         for n in (0, 1):
-            mine[d, n] = pair[n]
+            mine[d, n] = pair[n][d * slab : (d + 1) * slab]
     dq = dq_total[...].T.astype(jnp.bfloat16)
     for e in (1, 0):
         for g in range(group):
             start = e * half + g * rows
             dq_out[e, :, g * W : (g + 1) * W] = dq[start : start + rows, :]
-    dq_cols = query_grad.at[0, :, head_cols(head, wide)]
-    back[4] = remote(dq_out.at[1], dq_cols, back_send.at[4], back_recv.at[4], {"trunk": at[1]})
-    back[4].start()
-    kept.append(pltpu.make_async_copy(dq_out.at[0], dq_cols, local_sem.at[1]))
-    kept[1].start()
+    for e in (1, 0):
+        back[12 + e] = remote(
+            dq_out.at[e],
+            query_grad.at[0, :, head_cols(head, wide)],
+            back_send.at[12 + e],
+            back_recv.at[12 + e],
+            homes[e],
+        )
+        back[12 + e].start()
     for d in (3, 2, 1, 0):
         back[d].wait_recv()
         z_out[d] = (mine[d] + x_in[d].astype(jnp.float32)).astype(jnp.bfloat16)
-        if d == 0:
-            kept.append(pltpu.make_async_copy(z_out.at[0], z_in.at[0], local_sem.at[2]))
-            kept[2].start()
-        else:
-            back[8 + d] = remote(
-                z_out.at[d], z_in.at[d], back_send.at[8 + d], back_recv.at[8 + d], {"trunk": at[d]}
-            )
-            back[8 + d].start()
-    for d in (3, 2, 1):
-        back[4 + d].wait_recv()
-        back[8 + d].wait_recv()
-    back[4].wait_recv()
-    for copy in q_copies + sum(z_copies.values(), []) + sum(x_copies.values(), []):
+        back[8 + d] = remote(
+            z_out.at[d], z_in.at[d], back_send.at[8 + d], back_recv.at[8 + d], homes[d]
+        )
+        back[8 + d].start()
+    for key, copy in back.items():
+        if key >= 4:
+            copy.wait_recv()
+    limits.wait_send()
+    for copy in sum(z_copies.values(), []):
         copy.wait_send()
-    for copy in back.values():
-        copy.wait_send()
-    for copy in kept:
-        copy.wait()
+    for copies in (x_copies, back):
+        for copy in copies.values():
+            copy.wait_send()
 
 
 def owners_sum(
@@ -467,9 +452,11 @@
         in_specs=[smem] * 2 + [anywhere] * 6,
         out_specs=(anywhere,) * 3,
         scratch_shapes=[
-            pltpu.VMEM((2, rows, wide), bf16),
-            pltpu.VMEM((2, rows, wide), bf16),
-            pltpu.VMEM((2, 4, 2, slab, W), bf16),
+            pltpu.VMEM((2, 2, slab, W), bf16),
+            pltpu.VMEM((2, 2, rows, wide), bf16),
+            pltpu.VMEM((2, 2, rows, W), bf16),
+            pltpu.VMEM((2, 2, rows, wide), bf16),
+            pltpu.VMEM((2, 2, 4, slab, W), bf16),
             pltpu.VMEM((2, 4, rows, W), bf16),
             pltpu.VMEM((cols, W), bf16),
             pltpu.VMEM((cols, W), bf16),
@@ -482,13 +469,15 @@
             pltpu.VMEM((4, 2, slab, W), bf16),
             pltpu.VMEM((4, 2, rows, W), bf16),
             pltpu.VMEM((2, rows, wide), bf16),
-            dma((6,)),
-            dma((4, 4)),
-            dma((4, 4)),
-            dma((4, 2)),
-            dma((4, 2)),
+            pltpu.VMEM((2, 8, W), jnp.int32),
+            pltpu.VMEM((2, 8, W), jnp.int32),
             dma((12,)),
-            dma((12,)),
+            dma((4, 3)),
+            dma((4, 3)),
+            dma((4,)),
+            dma((4,)),
+            dma((14,)),
+            dma((14,)),
         ],
         compiler_params=pltpu.CompilerParams(
             collective_id=0, has_side_effects=True, vmem_limit_bytes=60 * 1024 * 1024
@@ -518,7 +507,7 @@
 
 
 def plan_of(mesh):
-    if mesh.shape["trunk"] == 4 and mesh.shape["branch"] == 2:
+    if mesh.shape["trunk"] == 4 and mesh.shape["branch"] == 2 and mesh.shape["tensor"] == 2:
         return fused
     return shards
 

time: 32.2 us -> 31.6 us (0.981)
  Pallas kernels: 30.1 us -> 29.5 us
    pallas_call x1, Pallas kernels: 28.4 us -> 27.7 us  [fused(): pl.pallas_call(fused_kernel, out_shape=(like(query), jax.ShapeDtypeStruct...]
where the time goes in v3:
time: 31.6 us; the launch traced here: 31.4 us
  Pallas kernels  29.5 us (93%)
  between operations  1.93 us (6%)
    pallas_call x1, Pallas kernels, fused(): pl.pallas_call(fused_kernel, out_shape=(like(query), jax.ShapeDtypeStruct...  27.7 us
    pallas_call x1, Pallas kernels, fused(): pl.pallas_call(owners_sum, out_shape=tuple((like(a) for a in (query, trun...  1.72 us

profile of v3, /device:TPU:0, one launch (start us, length us, event | category | flops | bytes accessed | tf_op | source)
XLA Modules:
  0.0 31.4 jit_solution(10342120463887533747)
XLA Ops:
  1.9 27.7 %shard_map.119 = (bf16[1,32,2048]{2,1,0:T(8,128)(2,1)}, bf16[4,2,128,128]{3,2,1,0:T(8,128)(2,1)}, bf16[4,2,32,128]{3,2,1,0:T(8,128)(2,1)}) custom-call(s32[1]{0:T(128)S(6)} %copy.13.forks, s32[1]{0:T(128)S(6)} %copy.14.lengths, bf16[1,32,2048]{2,1,0:T(8,128)(2,1)} %query.1, bf16[1,32,2048]{2,1,0:T(8,128)(2,1)} %cotangent.1, bf16[1,32,256]{2,1,0:T(8,128)(2,1)} %branch_keys.1, ...), custom_call_target="tpu_custom_call" | custom-call | flops 754974720 | bytes 1048576 | tf_op jit(solution)/shard_map/pallas_call | solution.py:445
  29.7 1.7 %shard_map.120 = (bf16[1,32,2048]{2,1,0:T(8,128)(2,1)}, bf16[128,256]{1,0:T(8,128)(2,1)}, bf16[128,256]{1,0:T(8,128)(2,1)}, bf16[1,32,256]{2,1,0:T(8,128)(2,1)}, bf16[1,32,256]{2,1,0:T(8,128)(2,1)}) custom-call(bf16[1,32,2048]{2,1,0:T(8,128)(2,1)} %get-tuple-element.8.query_in, bf16[4,2,128,128]{3,2,1,0:T(8,128)(2,1)} %get-tuple-element.9.z_in, ...), custom_call_target="tpu_custom_call" | custom-call | tf_op jit(solution)/shard_map/pallas_call | solution.py:498

commit v4 on v3

--- a/solution.py
+++ b/solution.py
@@ -258,7 +258,7 @@
     limits.start()
     for d in (1, 2, 3, 0):
         z_copies[d][0].start()
-    for d in (1, 2, 3, 0):
+    for d in (3, 1, 2, 0):
         z_copies[d][1].start()
     for d in (1, 0):
         z_copies[d][2].start()
@@ -340,6 +340,16 @@
         return dot(dscores, q_rows[...]), dot(low, c_rows[...])
 
     back = {}
+    pair = grads(own_base, own_rows, own_key)
+    for n in (0, 1):
+        mine_part = pair[n].astype(jnp.bfloat16)
+        for d in range(4):
+            own_out[d, n] = mine_part[d * rows : (d + 1) * rows, :]
+    for d in (3, 1, 2, 0):
+        back[4 + d] = remote(
+            own_out.at[d], own_in.at[d], back_send.at[4 + d], back_recv.at[4 + d], homes[d]
+        )
+        back[4 + d].start()
     for d in (3, 2, 1, 0):
         if d in (3, 1):
             key = kv[1, 0, d - 1 : d + 1].reshape(2 * slab, W)
@@ -349,16 +359,6 @@
             x_out[d, n] = part.astype(jnp.bfloat16)
         back[d] = remote(x_out.at[d], x_in.at[d], back_send.at[d], back_recv.at[d], twin)
         back[d].start()
-    pair = grads(own_base, own_rows, own_key)
-    for n in (0, 1):
-        mine_part = pair[n].astype(jnp.bfloat16)
-        for d in range(4):
-            own_out[d, n] = mine_part[d * rows : (d + 1) * rows, :]
-    for d in (3, 2, 1, 0):
-        back[4 + d] = remote(
-            own_out.at[d], own_in.at[d], back_send.at[4 + d], back_recv.at[4 + d], homes[d]
-        )
-        back[4 + d].start()
     pair = grads(0, 4 * slab, kv[0, 0].reshape(4 * slab, W))
     for d in range(4):
         for n in (0, 1):
@@ -377,7 +377,7 @@
             homes[e],
         )
         back[12 + e].start()
-    for d in (3, 2, 1, 0):
+    for d in (3, 1, 2, 0):
         back[d].wait_recv()
         z_out[d] = (mine[d] + x_in[d].astype(jnp.float32)).astype(jnp.bfloat16)
         back[8 + d] = remote(
@@ -404,18 +404,51 @@
     trunk_value_grad,
     branch_key_grad,
     branch_value_grad,
+    dq,
+    shares,
+    own_shares,
+    slabs,
+    branches,
+    sems,
 ):
     head = lax.rem(lax.axis_index("trunk"), 2)
     f32 = jnp.float32
-    query_grad[...] = query_in[...]
-    for a, b, which in ((0, 2, head), (1, 3, 1 - head)):
-        at = pl.ds(pl.multiple_of(which * W, W), W)
-        for n, ref in enumerate((trunk_key_grad, trunk_value_grad)):
-            ref[:, at] = (z_in[a, n].astype(f32) + z_in[b, n].astype(f32)).astype(jnp.bfloat16)
-        for n, ref in enumerate((branch_key_grad, branch_value_grad)):
-            ref[0, :, at] = (own_in[a, n].astype(f32) + own_in[b, n].astype(f32)).astype(
-                jnp.bfloat16
-            )
+    arrive = [
+        pltpu.make_async_copy(src, dst, sems.at[n])
+        for n, (src, dst) in enumerate(((query_in, dq), (z_in, shares), (own_in, own_shares)))
+    ]
+    results = (
+        (dq, query_grad),
+        (slabs.at[0], trunk_key_grad),
+        (slabs.at[1], trunk_value_grad),
+        (branches.at[0], branch_key_grad.at[0]),
+        (branches.at[1], branch_value_grad.at[0]),
+    )
+    leave = [
+        pltpu.make_async_copy(src, dst, sems.at[3 + n]) for n, (src, dst) in enumerate(results)
+    ]
+
+    def add(total, parts):
+        for a, b, which in ((0, 2, head), (1, 3, 1 - head)):
+            at = pl.ds(pl.multiple_of(which * W, W), W)
+            for n in (0, 1):
+                both = parts[a, n].astype(f32) + parts[b, n].astype(f32)
+                total[n, :, at] = both.astype(jnp.bfloat16)
+
+    for copy in arrive:
+        copy.start()
+    arrive[0].wait()
+    leave[0].start()
+    arrive[1].wait()
+    add(slabs, shares)
+    leave[1].start()
+    leave[2].start()
+    arrive[2].wait()
+    add(branches, own_shares)
+    leave[3].start()
+    leave[4].start()
+    for copy in leave:
+        copy.wait()
 
 
 def fused(
@@ -436,7 +469,6 @@
     bf16, f32 = jnp.bfloat16, jnp.float32
     smem = pl.BlockSpec(memory_space=pltpu.SMEM)
     anywhere = pl.BlockSpec(memory_space=pl.ANY)
-    vmem = pl.BlockSpec(memory_space=pltpu.VMEM)
 
     def like(a):
         return jax.ShapeDtypeStruct(a.shape, a.dtype)
@@ -500,8 +532,16 @@
         out_shape=tuple(
             like(a) for a in (query, trunk_keys, shared_trunk_values, branch_keys, rollout_value_rows)
         ),
-        in_specs=[vmem] * 3,
-        out_specs=(vmem,) * 5,
+        in_specs=[anywhere] * 3,
+        out_specs=(anywhere,) * 5,
+        scratch_shapes=[
+            pltpu.VMEM(query.shape, bf16),
+            pltpu.VMEM((4, 2, slab, W), bf16),
+            pltpu.VMEM((4, 2, rows, W), bf16),
+            pltpu.VMEM((2, slab, 2 * W), bf16),
+            pltpu.VMEM((2, rows, 2 * W), bf16),
+            dma((8,)),
+        ],
         compiler_params=pltpu.CompilerParams(vmem_limit_bytes=60 * 1024 * 1024),
     )(*shares)
 

time: 31.6 us -> 30.9 us (0.978)
  Pallas kernels: 29.5 us -> 28.8 us
    pallas_call x1, Pallas kernels: 27.7 us -> 27 us  [fused(): pl.pallas_call(fused_kernel, out_shape=(like(query), jax.ShapeDtypeStruct...]
where the time goes in v4:
time: 30.9 us; the launch traced here: 30.7 us
  Pallas kernels  28.8 us (93%)
  between operations  1.93 us (6%)
    pallas_call x1, Pallas kernels, fused(): pl.pallas_call(fused_kernel, out_shape=(like(query), jax.ShapeDtypeStruct...  27 us
    pallas_call x1, Pallas kernels, fused(): pl.pallas_call(owners_sum, out_shape=tuple((like(a) for a in (query, trun...  1.78 us

profile of v4, /device:TPU:0, one launch (start us, length us, event | category | flops | bytes accessed | tf_op | source)
XLA Modules:
  0.0 30.7 jit_solution(559394247053184963)
XLA Ops:
  1.9 27.0 %shard_map.119 = (bf16[1,32,2048]{2,1,0:T(8,128)(2,1)}, bf16[4,2,128,128]{3,2,1,0:T(8,128)(2,1)}, bf16[4,2,32,128]{3,2,1,0:T(8,128)(2,1)}) custom-call(s32[1]{0:T(128)S(6)} %copy.13.forks, s32[1]{0:T(128)S(6)} %copy.14.lengths, bf16[1,32,2048]{2,1,0:T(8,128)(2,1)} %query.1, bf16[1,32,2048]{2,1,0:T(8,128)(2,1)} %cotangent.1, bf16[1,32,256]{2,1,0:T(8,128)(2,1)} %branch_keys.1, ...), custom_call_target="tpu_custom_call" | custom-call | flops 754974720 | bytes 1048576 | tf_op jit(solution)/shard_map/pallas_call | solution.py:477
  28.9 1.8 %shard_map.120 = (bf16[1,32,2048]{2,1,0:T(8,128)(2,1)}, bf16[128,256]{1,0:T(8,128)(2,1)}, bf16[128,256]{1,0:T(8,128)(2,1)}, bf16[1,32,256]{2,1,0:T(8,128)(2,1)}, bf16[1,32,256]{2,1,0:T(8,128)(2,1)}) custom-call(bf16[1,32,2048]{2,1,0:T(8,128)(2,1)} %get-tuple-element.8.query_in, bf16[4,2,128,128]{3,2,1,0:T(8,128)(2,1)} %get-tuple-element.9.z_in, ...), custom_call_target="tpu_custom_call" | custom-call | tf_op jit(solution)/shard_map/pallas_call | solution.py:530
